TPU v7x, 256 devices: a whole 4x4x8 slice. The times are simulated.
256 devices in a mesh: seq: 16 (over x, y_hi, core), dp: 16 (over z, y_lo).
Axes of the slice: x: 4, y: 4 (y_hi: 2, y_lo: 2; y = y_hi * 2 + y_lo), z: 8, core: 2. Of those that a mesh axis runs over, the one named last changes fastest.
Arguments:
- frames: bfloat16 [16, 2048, 1024], P('dp', 'seq'), may hold values from -6 to 6
- lengths: int32 [16], P('dp'), may hold values from 1024 to 2048, as said below
- stretch_sizes: int32 [16], P('dp'), may hold values from 8 to 32, as said below
- look_ahead: int32 [16], P('dp'), may hold values from 1 to 8, as said below
- norm_one: float32 [1024], replicated, may hold values from 0.5 to 1.5
- norm_two: float32 [1024], replicated, may hold values from 0.5 to 1.5
- w_query: bfloat16 [1024, 1024], replicated, may hold values from -8 to 8
- w_key: bfloat16 [1024, 1024], replicated, may hold values from -1 to 1
- w_value: bfloat16 [1024, 1024], replicated, may hold values from -0.1875 to 0.1875
- w_out: bfloat16 [1024, 1024], replicated, may hold values from -0.1875 to 0.1875
- conv_kernel: bfloat16 [31, 1024], replicated, may hold values from -1 to 1
Outputs:
- full_output: bfloat16 [16, 2048, 1024], P('dp', 'seq')
- stretch_output: bfloat16 [16, 2048, 1024], P('dp', 'seq')
- kernel_grad: float32 [31, 1024], replicated
Inputs may be any that keep to these rules, and one draw needn't show every extreme that they name: `lengths`: utterance 0 has all 2048 frames. `stretch_sizes`: utterance 0 has stretch size 32. `look_ahead`: utterance 0 has preview 8.
All inputs are finite; a program needn't handle non-finite values.
Results may differ from a plain program's by a relative error of at most 0.0045.
The roundings to bfloat16 on the way count: a program that leaves them out, or rounds other values in their place, can miss the bound.
Values may be sent and summed in bfloat16 or wider, within the bound.
No kernel may reach another device: no remote copies, remote signals or barrier semaphores. Data moves between devices by JAX's collectives and lax.ppermute only.
A program may use at most 128 MiB of HBM per device.

v0:
```python
import math
import jax
import jax.numpy as jnp
from jax import lax
from jax.sharding import PartitionSpec as P

HEADS = 16
KERNEL = 31
LEFT = 64
HALO = 128
EPSILON = 1e-05
FLOOR_SCORE = -1e30


def with_halo(value, sides, width):
    for axis, dim in sides:
        size, length = (lax.axis_size(axis), value.shape[dim])
        up = [(i, (i + 1) % size) for i in range(size - 1)]
        down = [(j, i) for i, j in up]
        last = lax.slice_in_dim(value, length - width, length, axis=dim)
        leading = lax.slice_in_dim(value, 0, width, axis=dim)
        before = lax.ppermute(last, axis, up)
        after = lax.ppermute(leading, axis, down)
        value = jnp.concatenate([before, value, after], axis=dim)
    return value


def shifted(value, axis, by):
    length = lax.axis_size(axis)
    pairs = [(i, i + by) for i in range(length) if 0 <= i + by < length]
    return lax.ppermute(value, axis, pairs)


def layer_norm(values, gain_vector):
    values = values.astype(jnp.float32)
    center = values - jnp.mean(values, axis=-1, keepdims=True)
    spread = jnp.mean(center * center, axis=-1, keepdims=True)
    return center * lax.rsqrt(spread + EPSILON) * gain_vector


def fresh_state(row_count, head_count, depth_count):
    return (
        jnp.full((head_count, row_count), FLOOR_SCORE, jnp.float32),
        jnp.zeros((head_count, row_count), jnp.float32),
        jnp.zeros((row_count, head_count * depth_count), jnp.float32),
    )


def finish_state(state):
    highest, totals, summed = state
    row_count = summed.shape[0]
    head_count = totals.shape[0]
    mixed = summed.reshape(row_count, head_count, -1) / totals.T[:, :, None]
    return mixed.reshape(row_count, -1).astype(jnp.bfloat16)


def fold_keys(state, query3, query_pos, key3, value3, key_start, length, scale):
    highest, totals, summed = state
    key_count = key3.shape[0]
    scores = jnp.einsum("qhe,khe->hqk", query3, key3, preferred_element_type=jnp.float32) * scale
    key_pos = key_start + jnp.arange(key_count, dtype=jnp.int32)
    visible = (key_pos[None, :] < length) | (key_pos[None, :] == query_pos[:, None])
    scores = jnp.where(visible[None], scores, FLOOR_SCORE)
    new_high = jnp.maximum(highest, jnp.max(scores, axis=-1))
    factor = jnp.exp(highest - new_high)
    expo = jnp.where(visible[None], jnp.exp(scores - new_high[:, :, None]), 0.0)
    totals = totals * factor + jnp.sum(expo, axis=-1)
    adding = jnp.einsum(
        "hqk,khe->qhe", expo.astype(jnp.bfloat16), value3, preferred_element_type=jnp.float32
    )
    row_count, head_count, depth_count = adding.shape
    summed = summed.reshape(row_count, head_count, depth_count) * factor.T[:, :, None] + adding
    return (new_high, totals, summed.reshape(row_count, head_count * depth_count))


def fold_blocks(state, query3, query_pos, keys3, values3, length, scale):
    key_count = keys3.shape[0]
    block_width = math.gcd(key_count, 256)
    number = key_count // block_width
    key_blocks = keys3.reshape(number, block_width, keys3.shape[1], keys3.shape[2])
    value_blocks = values3.reshape(number, block_width, values3.shape[1], values3.shape[2])

    def advance(carry, inputs):
        index, key_block, value_block = inputs
        return (
            fold_keys(
                carry, query3, query_pos, key_block, value_block, index * block_width, length, scale
            ),
            None,
        )

    state, _ = lax.scan(
        advance, state, (jnp.arange(number, dtype=jnp.int32), key_blocks, value_blocks)
    )
    return state


def windowed(query3, key_ext3, value_ext3, first_pos, length, stretch, lookup, scale):
    query_count = query3.shape[0]
    block_rows = min(query_count, 512)
    number = query_count // block_rows
    span = block_rows + 2 * HALO

    def one_block(index):
        start = index * block_rows
        query_pos = first_pos + start + jnp.arange(block_rows, dtype=jnp.int32)
        key_pos = first_pos + start - HALO + jnp.arange(span, dtype=jnp.int32)
        begin = query_pos // stretch * stretch
        inside = (key_pos[None, :] >= begin[:, None] - LEFT) & (
            key_pos[None, :] < begin[:, None] + stretch + lookup
        )
        inside = inside & (key_pos[None, :] >= 0) & (key_pos[None, :] < length)
        visible = inside | (key_pos[None, :] == query_pos[:, None])
        scores = (
            jnp.einsum("qhe,khe->hqk", query3, key_ext3, preferred_element_type=jnp.float32) * scale
        )
        scores = jnp.where(visible[None], scores, FLOOR_SCORE)
        highest = jnp.max(scores, axis=-1, keepdims=True)
        expo = jnp.where(visible[None], jnp.exp(scores - highest), 0.0)
        totals = jnp.sum(expo, axis=-1)
        mixed = jnp.einsum(
            "hqk,khe->qhe",
            expo.astype(jnp.bfloat16),
            value_ext3,
            preferred_element_type=jnp.float32,
        )
        return (mixed / totals.T[:, :, None]).reshape(block_rows, -1).astype(jnp.bfloat16)

    return lax.map(one_block, jnp.arange(number, dtype=jnp.int32)).reshape(query_count, -1)


def per_device(
    frames,
    lengths,
    stretch_sizes,
    look_ahead,
    norm_one,
    norm_two,
    w_query,
    w_key,
    w_value,
    w_out,
    conv_kernel,
):
    source = frames[0]
    row_count, model_width = source.shape
    head_count = HEADS
    depth_count = model_width // head_count
    scale = float(depth_count) ** (-0.5)
    seq_place = lax.axis_index("seq")
    length = lengths[0]
    stretch = stretch_sizes[0]
    lookup = look_ahead[0]
    first_pos = seq_place * row_count
    query_pos = first_pos + jnp.arange(row_count, dtype=jnp.int32)
    normed = layer_norm(source, norm_one).astype(jnp.bfloat16)
    query = jnp.dot(normed, w_query, preferred_element_type=jnp.float32).astype(jnp.bfloat16)
    key_rows = jnp.dot(normed, w_key, preferred_element_type=jnp.float32).astype(jnp.bfloat16)
    value_rows = jnp.dot(normed, w_value, preferred_element_type=jnp.float32).astype(jnp.bfloat16)
    query3 = query.reshape(row_count, head_count, depth_count)
    key_piece = lax.all_gather(key_rows, "seq", axis=0, tiled=True)
    value_piece = lax.all_gather(value_rows, "seq", axis=0, tiled=True)
    piece_rows = key_piece.shape[0]
    state = fold_blocks(
        fresh_state(row_count, head_count, depth_count),
        query3,
        query_pos,
        key_piece.reshape(piece_rows, head_count, depth_count),
        value_piece.reshape(piece_rows, head_count, depth_count),
        length,
        scale,
    )
    context_full = finish_state(state)
    stacked = jnp.stack([key_rows, value_rows])
    extended = with_halo(stacked, (("seq", 1),), HALO)
    context_stretch = windowed(
        query3,
        extended[0].reshape(-1, head_count, depth_count),
        extended[1].reshape(-1, head_count, depth_count),
        first_pos,
        length,
        stretch,
        lookup,
        scale,
    )
    valid = (query_pos < length).astype(jnp.float32)
    kernel_taps = conv_kernel.astype(jnp.float32)
    projected = jnp.dot(
        jnp.concatenate([context_full, context_stretch], axis=0),
        w_out,
        preferred_element_type=jnp.float32,
    )
    residual_full = source.astype(jnp.float32) + projected[:row_count]
    residual_stretch = source.astype(jnp.float32) + projected[row_count:]
    input_full = (layer_norm(residual_full, norm_two) * valid[:, None]).astype(jnp.bfloat16)
    input_stretch = (layer_norm(residual_stretch, norm_two) * valid[:, None]).astype(jnp.bfloat16)
    padded_full = with_halo(input_full, (("seq", 0),), KERNEL // 2)
    carried = shifted(input_stretch[row_count - (KERNEL - 1) :], "seq", 1)
    padded_stretch = jnp.concatenate([carried, input_stretch], axis=0)
    conv_full = jnp.zeros((row_count, model_width), jnp.float32)
    conv_stretch = jnp.zeros((row_count, model_width), jnp.float32)
    for offset in range(KERNEL):
        conv_full = conv_full + kernel_taps[offset] * padded_full[
            offset : offset + row_count
        ].astype(jnp.float32)
        conv_stretch = conv_stretch + kernel_taps[offset] * padded_stretch[
            offset : offset + row_count
        ].astype(jnp.float32)
    output_full = residual_full + jax.nn.silu(conv_full)
    output_stretch = residual_stretch + jax.nn.silu(conv_stretch)
    push = (
        2.0 * (output_stretch - output_full) * valid[:, None] / jnp.sqrt(length.astype(jnp.float32))
    )
    sigma = jax.nn.sigmoid(conv_stretch)
    slope = push * sigma * (1.0 + conv_stretch * (1.0 - sigma))
    grad_local = jnp.stack(
        [
            jnp.sum(slope * padded_stretch[offset : offset + row_count].astype(jnp.float32), axis=0)
            for offset in range(KERNEL)
        ]
    )
    kernel_grad = lax.psum(grad_local, ("seq", "dp"))
    return (
        output_full.astype(jnp.bfloat16)[None],
        output_stretch.astype(jnp.bfloat16)[None],
        kernel_grad,
    )


def solution(mesh):
    in_specs = (P("dp", "seq", None), P("dp"), P("dp"), P("dp"), P(), P(), P(), P(), P(), P(), P())
    out_specs = (P("dp", "seq", None), P("dp", "seq", None), P())
    return jax.shard_map(
        per_device, mesh=mesh, in_specs=in_specs, out_specs=out_specs, check_vma=False
    )
```

profile of v0, /device:TPU:8, one launch (start us, length us, event | category | flops | bytes accessed | tf_op | source)
XLA Modules:
  0.0 529.4 jit_solution(953079403688141178)
XLA Ops:
  7.2 1.2 convert_reduce_fusion
  8.5 1.2 fusion.44
  9.7 2.9 convolution_convert_fusion.2
  12.7 2.8 convolution_convert_fusion
  15.6 1.9 pad_maximum_fusion.1
  17.4 2.6 collective-permute-start
  20.0 1.3 collective-permute-start.1
  23.2 2.1 convolution_convert_fusion.1
  27.8 1.4 pad_maximum_fusion
  29.2 1.0 fusion.184
  30.2 2.3 copy.28
  32.5 1.2 copy.27
  33.6 3.8 fusion.188
  37.4 2.9 fusion.36
  40.3 40.4 %all-gather.3.cloned.1.call-done = bf16[2048,1024]{1,0:T(8,128)(2,1)} async-done(((bf16[128,1024]{1,0:T(8,128)(2,1)}), bf16[2048,1024]{1,0:T(8,128)(2,1)}) %all-gather.3.cloned.1.call-update) | async-done | bytes 4194320 | tf_op jit(solution)/shard_map/all_gather | solution.py:161
  80.8 11.6 %reshape.276 = bf16[8,256,16,64]{3,2,1,0:T(8,128)(2,1)} reshape(bf16[2048,1024]{1,0:T(8,128)(2,1)} %all-gather.3.cloned.1.call-done) | data formatting | bytes 8388608 | tf_op jit(solution)/shard_map/reshape;reshape | solution.py:80
  92.3 10.4 %copy.25 = bf16[8,256,16,64]{1,3,2,0:T(8,128)(2,1)} copy(bf16[8,256,16,64]{3,2,1,0:T(8,128)(2,1)} %reshape.276) | data formatting | bytes 8388608
  102.7 41.3 %all-gather.5.cloned.1.call-done = bf16[2048,1024]{1,0:T(8,128)(2,1)} async-done(((bf16[128,1024]{1,0:T(8,128)(2,1)}), bf16[2048,1024]{1,0:T(8,128)(2,1)}) %all-gather.5.cloned.1.call-update) | async-done | bytes 4194320 | tf_op jit(solution)/shard_map/all_gather | solution.py:162
  144.0 11.6 %reshape.277 = bf16[8,256,16,64]{3,2,1,0:T(8,128)(2,1)} reshape(bf16[2048,1024]{1,0:T(8,128)(2,1)} %all-gather.5.cloned.1.call-done) | data formatting | bytes 8388608 | tf_op jit(solution)/shard_map/reshape;reshape | solution.py:81
  155.6 10.3 %copy.26 = bf16[8,256,16,64]{1,3,2,0:T(8,128)(2,1)} copy(bf16[8,256,16,64]{3,2,1,0:T(8,128)(2,1)} %reshape.277) | data formatting | bytes 8388608
  166.0 65.6 %while.5 = (s32[]{:T(128)}, f32[16,128]{1,0:T(8,128)S(1)}, f32[16,128]{1,0:T(8,128)S(1)}, f32[128,1024]{0,1:T(8,128)S(1)}, s32[8]{0:T(128)S(1)}, /*index=5*/s32[...) while((s32[]{:T(128)}, f32[16,128]{1,0:T(8,128)S(1)}, ...), condition=%wide.region_5.6_spmd.clone, body=%wide.region_2.5_spmd.clone.sunk | while | flops 141374336 | bytes 17306316 | solution.py:92
  168.0 2.9 fusion.211
  171.0 2.6 fusion.215
  176.2 2.9 fusion.211
  179.2 2.6 fusion.215
  184.4 2.9 fusion.211
  187.4 2.6 fusion.215
  192.6 2.9 fusion.211
  195.6 2.6 fusion.215
  200.8 2.9 fusion.211
  203.8 2.6 fusion.215
  209.0 2.9 fusion.211
  212.0 2.6 fusion.215
  217.2 2.9 fusion.211
  220.2 2.6 fusion.215
  225.4 2.9 fusion.211
  228.4 2.6 fusion.215
  231.6 1.7 fusion.108
  235.0 2.2 collective-permute-start.4
  237.8 3.8 collective-permute-start.2
  241.6 1.3 collective-permute-start.3
  243.5 1.5 collective-permute-done.3
  245.1 21.2 %fusion.106 = (f32[1024]{0:T(1024)S(1)}, f32[1024]{0:T(1024)S(1)}, f32[1024]{0:T(1024)S(1)}, f32[1024]{0:T(1024)S(1)}, f32[1024]{0:T(1024)S(1)}, /*index=5*/f32[...) fusion(bf16[128,1024]{1,0:T(8,128)(2,1)} %copy-done.3, ...), kind=kLoop, calls=%fused_computation.235 | loop fusion | flops 57138176 | bytes 3432964 | tf_op jit(solution)/shard_map/reduce_sum | solution.py:218
  266.9 1.3 fusion.83
  269.0 4.7 stack.139
  273.8 1.9 convert_bitcast_fusion.1
  275.7 245.6 %all-reduce.2.cloned.1.call-done = f32[31,1024]{1,0:T(8,128)} async-done(((f32[31,1024]{1,0:T(8,128)}), f32[31,1024]{1,0:T(8,128)}) %all-reduce.2.cloned.1.call-update) | async-done | bytes 126992 | tf_op jit(solution)/shard_map/psum | solution.py:222
  521.3 1.6 copy.50
  (150 shorter events, 22.5 us)
Async XLA Ops:
  7.2 224.5 %copy-start = (bf16[1024,1024]{1,0:T(8,128)(2,1)S(1)}, bf16[1024,1024]{1,0:T(8,128)(2,1)}, u32[]{:S(2)}) copy-start(bf16[1024,1024]{1,0:T(8,128)(2,1)} %param.22) | copy-start | bytes 6291460
  7.2 5.5 %copy-start.2 = (bf16[1,128,1024]{2,1,0:T(8,128)(2,1)S(1)}, bf16[1,128,1024]{2,1,0:T(8,128)(2,1)}, u32[]{:S(2)}) copy-start(bf16[1,128,1024]{2,1,0:T(8,128)(2,1)} %param.13) | copy-start | bytes 786436
  7.2 5.5 %copy-start.10 = (f32[1024]{0:T(1024)S(1)}, f32[1024]{0:T(1024)}, u32[]{:S(2)}) copy-start(f32[1024]{0:T(1024)} %param.17) | copy-start | bytes 12292
  7.2 73.6 %all-gather.3.cloned.1.call-start = ((), (), s32[]{:S(2)}) async-start(), calls=%async_computation | async-start | bytes 4456448 | tf_op jit(solution)/shard_map/all_gather | solution.py:161
  12.6 3.0 copy-start.5
  12.6 131.4 %all-gather.5.cloned.1.call-start = ((), (), s32[]{:S(2)}) async-start(), calls=%async_computation.1 | async-start | bytes 4456448 | tf_op jit(solution)/shard_map/all_gather | solution.py:162
  15.5 505.8 %all-reduce.2.cloned.1.call-start = ((), (), s32[]{:S(2)}) async-start(), calls=%async_computation.2 | async-start | bytes 262144 | tf_op jit(solution)/shard_map/psum | solution.py:222
  15.5 10.9 %copy-start.9 = (bf16[31,1024]{1,0:T(8,128)(2,1)S(1)}, bf16[31,1024]{1,0:T(8,128)(2,1)}, u32[]{:S(2)}) copy-start(bf16[31,1024]{1,0:T(8,128)(2,1)} %param.23) | copy-start | bytes 190468
  15.5 12.3 %copy-start.6 = (bf16[128,1024]{1,0:T(8,128)(2,1)S(1)}, bf16[128,1024]{1,0:T(8,128)(2,1)}, u32[]{:S(2)}) copy-start(bf16[128,1024]{1,0:T(8,128)(2,1)} %convolution_convert_fusion) | copy-start | bytes 786436
  17.4 10.4 %collective-permute-start = (bf16[2,128,1024]{2,1,0:T(8,128)(2,1)}, bf16[2,128,1024]{2,1,0:T(8,128)(2,1)}, u32[]{:S(2)}, u32[]{:S(2)}) collective-permute-start(bf16[2,128,1024]{2,1,0:T(8,128)(2,1)} %pad_maximum_fusion.1), channel_id=1, source_target_pairs={{0,16},{16,32},{32,48},{48,64},{64,80},{80,96},{96,112},{112,128},... | collective-permute-start | bytes 1572872 | tf_op jit(solution)/shard_map/ppermute | solution.py:22
  20.0 7.8 %collective-permute-start.1 = (bf16[2,128,1024]{2,1,0:T(8,128)(2,1)}, bf16[2,128,1024]{2,1,0:T(8,128)(2,1)}, u32[]{:S(2)}, u32[]{:S(2)}) collective-permute-start(bf16[2,128,1024]{2,1,0:T(8,128)(2,1)} %pad_maximum_fusion.1), channel_id=1, source_target_pairs={{16,0},{32,16},{48,32},{64,48},{80,64},{96,80},{112,96},{128,112},... | collective-permute-start | bytes 1572872 | tf_op jit(solution)/shard_map/ppermute | solution.py:23
  33.6 3.8 copy-start.8
  171.0 2.6 copy-start.1
  179.2 2.6 copy-start.1
  187.4 2.6 copy-start.1
  195.6 2.6 copy-start.1
  203.8 2.6 copy-start.1
  212.0 2.6 copy-start.1
  220.2 2.6 copy-start.1
  228.4 2.6 copy-start.1
  233.3 0.7 copy-start.11
  233.3 0.7 copy-start.12
  234.3 0.7 copy-start.3
  234.3 2.9 copy-start.7
  235.0 10.0 %collective-permute-start.4 = (bf16[30,1024]{1,0:T(8,128)(2,1)S(1)}, bf16[30,1024]{1,0:T(8,128)(2,1)S(1)}, u32[]{:S(2)}, u32[]{:S(2)}) collective-permute-start(bf16[30,1024]{1,0:T(8,128)(2,1)S(1)} %slice.576), channel_id=1, source_target_pairs={{0,16},{16,32},{32,48},{48,64},{64,80},{80,96},{96,112},{112,128},... | collective-permute-start | bytes 184328 | tf_op jit(solution)/shard_map/ppermute | solution.py:31
  237.8 5.7 %collective-permute-start.2 = (bf16[15,1024]{1,0:T(8,128)(2,1)}, bf16[15,1024]{1,0:T(8,128)(2,1)}, u32[]{:S(2)}, u32[]{:S(2)}) collective-permute-start(bf16[15,1024]{1,0:T(8,128)(2,1)} %get-tuple-element.207), channel_id=1, source_target_pairs={{0,16},{16,32},{32,48},{48,64},{64,80},{80,96},{96,112},{112,128},... | collective-permute-start | bytes 92168 | tf_op jit(solution)/shard_map/ppermute | solution.py:22
  241.6 3.4 collective-permute-start.3
  243.5 22.7 %copy-start.4 = (bf16[128,1024]{1,0:T(8,128)(2,1)S(1)}, bf16[128,1024]{1,0:T(8,128)(2,1)}, u32[]{:S(2)}) copy-start(bf16[128,1024]{1,0:T(8,128)(2,1)} %copy-done.3) | copy-start | bytes 786436
Sparse Core Ops, SparseCore 0:
  12.7 67.9 all-gather.2
  84.0 59.9 all-gather.4
  273.9 247.2 all-reduce.1
where the time goes:
time: 532 us; the launch traced here: 529 us
  waiting for transfers between devices  329 us (62%)
  local copies, waits for them, and re-layouts  62.4 us (12%)
  matrix products  60.6 us (11%)
  other arithmetic  44.4 us (8%)
  between operations  16.1 us (3%)
  starting transfers between devices  11.2 us (2%)
  loops' own time  5.82 us (1%)
    psum x1, waiting for transfers between devices, per_device(): kernel_grad = lax.psum(grad_local, ('seq', 'dp'))  246 us
    all_gather x1, waiting for transfers between devices, per_device(): value_piece = lax.all_gather(value_rows, 'seq', axis=0, tiled=True)  41.3 us
    all_gather x1, waiting for transfers between devices, per_device(): key_piece = lax.all_gather(key_rows, 'seq', axis=0, tiled=True)  40.4 us
    reduce_sum x4, other arithmetic, per_device(): jnp.sum(slope * padded_stretch[offset:offset + row_count].astype(jnp.floa...  24 us
    dot_general x8, matrix products, fold_keys(): jnp.einsum('qhe,khe->hqk', query3, key3, preferred_element_type=jnp.float32)  23.4 us
    unnamed x27, local copies, waits for them, and re-layouts  23.2 us
    dot_general x8, matrix products, fold_keys(): jnp.einsum('hqk,khe->qhe', expo.astype(jnp.bfloat16), value3, preferred_e...  21 us
    another operation x1, local copies, waits for them, and re-layouts, fold_blocks(): values3.reshape(number, block_width, values3.shape[1], values3.shape[2])  11.6 us
  transfers between devices with their start and end apart: 8, of which 4 were waited for; matrix products, arithmetic and copies ran while one was open for 9% of the time, Pallas kernels for 0%

commit v1 on v0

--- a/solution.py
+++ b/solution.py
@@ -219,7 +219,7 @@
             for offset in range(KERNEL)
         ]
     )
-    kernel_grad = lax.psum(grad_local, ("seq", "dp"))
+    kernel_grad = jnp.sum(lax.all_gather(grad_local, ("seq", "dp")), axis=0)
     return (
         output_full.astype(jnp.bfloat16)[None],
         output_stretch.astype(jnp.bfloat16)[None],

time: 532 us -> 1040 us (1.95)
  the two profiles are of different devices: /device:TPU:8 before, /device:TPU:99 now
where the time goes in v1:
time: 1040 us
  waiting for transfers between devices  840 us (81%)
  local copies, waits for them, and re-layouts  60.2 us (6%)
  other arithmetic  57.5 us (6%)
  matrix products  43.2 us (4%)
  starting transfers between devices  16.9 us (2%)
  between operations  16.1 us (2%)
    all_gather x1, waiting for transfers between devices, per_device(): kernel_grad = jnp.sum(lax.all_gather(grad_local, ('seq', 'dp')), axis=0)  761 us
    all_gather x1, waiting for transfers between devices, per_device(): value_piece = lax.all_gather(value_rows, 'seq', axis=0, tiled=True)  41.3 us
    all_gather x1, waiting for transfers between devices, per_device(): key_piece = lax.all_gather(key_rows, 'seq', axis=0, tiled=True)  29.3 us
    reduce_sum x4, other arithmetic, per_device(): jnp.sum(slope * padded_stretch[offset:offset + row_count].astype(jnp.floa...  24.4 us
    unnamed x26, local copies, waits for them, and re-layouts  21.7 us
  transfers between devices with their start and end apart: 8, of which 6 were waited for; matrix products, arithmetic and copies ran while one was open for 4% of the time, Pallas kernels for 0%

profile of v1, /device:TPU:99, one launch (start us, length us, event | category | flops | bytes accessed | tf_op | source)
XLA Modules:
  0.0 1039.9 jit_solution(4578764949552929264)
XLA Ops:
  7.2 1.2 convert_reduce_fusion
  8.5 1.2 fusion.44
  9.7 2.9 convolution_convert_fusion.2
  12.7 2.8 convolution_convert_fusion
  15.6 1.9 pad_maximum_fusion.1
  17.4 2.6 collective-permute-start.1
  20.0 4.7 collective-permute-start
  26.7 2.2 convolution_convert_fusion.1
  31.3 1.8 collective-permute-done.1
  33.1 5.4 collective-permute-done
  38.6 1.3 pad_maximum_fusion
  40.9 2.3 copy.36
  44.4 3.8 fusion.188
  48.1 2.9 fusion.36
  51.0 29.3 %all-gather.6.cloned.1.call-done = bf16[2048,1024]{1,0:T(8,128)(2,1)} async-done(((bf16[128,1024]{1,0:T(8,128)(2,1)}), bf16[2048,1024]{1,0:T(8,128)(2,1)}) %all-gather.6.cloned.1.call-update) | async-done | bytes 4194320 | tf_op jit(solution)/shard_map/all_gather | solution.py:161
  80.3 11.6 %reshape.280 = bf16[8,256,16,64]{3,2,1,0:T(8,128)(2,1)} reshape(bf16[2048,1024]{1,0:T(8,128)(2,1)} %all-gather.6.cloned.1.call-done) | data formatting | bytes 8388608 | tf_op jit(solution)/shard_map/reshape;reshape | solution.py:80
  91.9 10.4 copy.33
  102.2 41.3 %all-gather.8.cloned.1.call-done = bf16[2048,1024]{1,0:T(8,128)(2,1)} async-done(((bf16[128,1024]{1,0:T(8,128)(2,1)}), bf16[2048,1024]{1,0:T(8,128)(2,1)}) %all-gather.8.cloned.1.call-update) | async-done | bytes 4194320 | tf_op jit(solution)/shard_map/all_gather | solution.py:162
  143.6 11.6 %reshape.281 = bf16[8,256,16,64]{3,2,1,0:T(8,128)(2,1)} reshape(bf16[2048,1024]{1,0:T(8,128)(2,1)} %all-gather.8.cloned.1.call-done) | data formatting | bytes 8388608 | tf_op jit(solution)/shard_map/reshape;reshape | solution.py:81
  155.2 10.3 copy.34
  165.5 48.2 %while.5 = (s32[]{:T(128)}, f32[16,128]{1,0:T(8,128)S(1)}, f32[16,128]{1,0:T(8,128)S(1)}, f32[128,1024]{0,1:T(8,128)S(1)}, s32[8]{0:T(128)S(1)}, /*index=5*/s32[...) while((s32[]{:T(128)}, f32[16,128]{1,0:T(8,128)S(1)}, ...), condition=%wide.region_5.6_spmd.clone, body=%wide.region_2.5_spmd.clone.sunk | while | flops 141374336 | bytes 8916672 | solution.py:92
  167.6 1.6 fusion.211
  169.7 1.8 fusion.215
  173.6 1.6 fusion.211
  175.7 1.8 fusion.215
  179.6 1.6 fusion.211
  181.8 1.8 fusion.215
  185.7 1.6 fusion.211
  187.8 1.8 fusion.215
  191.7 1.6 fusion.211
  193.8 1.8 fusion.215
  197.7 1.6 fusion.211
  199.8 1.8 fusion.215
  203.7 1.6 fusion.211
  205.9 1.8 fusion.215
  209.8 1.6 fusion.211
  211.9 1.8 fusion.215
  213.8 1.7 fusion.108
  217.9 2.2 collective-permute-start.2
  220.1 2.3 collective-permute-start.3
  222.4 5.0 collective-permute-start.4
  228.9 21.6 %fusion.106 = (f32[1024]{0:T(1024)S(1)}, f32[1024]{0:T(1024)S(1)}, f32[1024]{0:T(1024)S(1)}, f32[1024]{0:T(1024)S(1)}, f32[1024]{0:T(1024)S(1)}, /*index=5*/f32[...) fusion(bf16[128,1024]{1,0:T(8,128)(2,1)} %copy-done.2, ...), kind=kLoop, calls=%fused_computation.235 | loop fusion | flops 57138176 | bytes 3432964 | tf_op jit(solution)/shard_map/reduce_sum | solution.py:218
  250.8 1.3 fusion.92
  252.0 1.3 fusion.83
  253.3 4.1 stack.139
  257.4 1.9 convert_bitcast_fusion.1
  259.3 761.3 %all-gather.10.cloned.1.call-done = f32[256,31,1024]{2,1,0:T(8,128)} async-done(((f32[1,31,1024]{2,1,0:T(8,128)}), f32[256,31,1024]{2,1,0:T(8,128)}) %all-gather.10.cloned.1.call-update) | async-done | bytes 32505872 | tf_op jit(solution)/shard_map/all_gather | solution.py:222
  1020.6 12.8 %reduce_sum.399 = f32[31,1024]{1,0:T(8,128)} reduce(f32[256,31,1024]{2,1,0:T(8,128)} %all-gather.10.cloned.1.call-done, f32[]{:T(128)} %constant.75.clone.1), dimensions={0}, to_apply=%region_43.44 | reduce | flops 8094720 | bytes 32632836 | tf_op jit(solution)/shard_map/reduce_sum | solution.py:222
  (134 shorter events, 24.3 us)
Async XLA Ops:
  7.2 206.6 %copy-start = (bf16[1024,1024]{1,0:T(8,128)(2,1)S(1)}, bf16[1024,1024]{1,0:T(8,128)(2,1)}, u32[]{:S(2)}) copy-start(bf16[1024,1024]{1,0:T(8,128)(2,1)} %param.22) | copy-start | bytes 6291460
  7.2 5.5 copy-start.1
  7.2 5.5 copy-start.9
  7.2 73.1 %all-gather.6.cloned.1.call-start = ((), (), s32[]{:S(2)}) async-start(), calls=%async_computation | async-start | bytes 4456448 | tf_op jit(solution)/shard_map/all_gather | solution.py:161
  12.6 3.0 copy-start.4
  12.6 131.0 %all-gather.8.cloned.1.call-start = ((), (), s32[]{:S(2)}) async-start(), calls=%async_computation.1 | async-start | bytes 4456448 | tf_op jit(solution)/shard_map/all_gather | solution.py:162
  15.5 1005.1 %all-gather.10.cloned.1.call-start = ((), (), s32[]{:S(2)}) async-start(), calls=%async_computation.2 | async-start | bytes 33685504 | tf_op jit(solution)/shard_map/all_gather | solution.py:222
  15.5 14.5 %copy-start.8 = (bf16[31,1024]{1,0:T(8,128)(2,1)S(1)}, bf16[31,1024]{1,0:T(8,128)(2,1)}, u32[]{:S(2)}) copy-start(bf16[31,1024]{1,0:T(8,128)(2,1)} %param.23) | copy-start | bytes 190468
  15.5 23.0 %copy-start.5 = (bf16[128,1024]{1,0:T(8,128)(2,1)S(1)}, bf16[128,1024]{1,0:T(8,128)(2,1)}, u32[]{:S(2)}) copy-start(bf16[128,1024]{1,0:T(8,128)(2,1)} %convolution_convert_fusion) | copy-start | bytes 786436
  17.4 15.7 %collective-permute-start.1 = (bf16[2,128,1024]{2,1,0:T(8,128)(2,1)}, bf16[2,128,1024]{2,1,0:T(8,128)(2,1)}, u32[]{:S(2)}, u32[]{:S(2)}) collective-permute-start(bf16[2,128,1024]{2,1,0:T(8,128)(2,1)} %pad_maximum_fusion.1), channel_id=1, source_target_pairs={{16,0},{32,16},{48,32},{64,48},{80,64},{96,80},{112,96},{128,112},... | collective-permute-start | bytes 1572872 | tf_op jit(solution)/shard_map/ppermute | solution.py:23
  20.0 18.6 %collective-permute-start = (bf16[2,128,1024]{2,1,0:T(8,128)(2,1)}, bf16[2,128,1024]{2,1,0:T(8,128)(2,1)}, u32[]{:S(2)}, u32[]{:S(2)}) collective-permute-start(bf16[2,128,1024]{2,1,0:T(8,128)(2,1)} %pad_maximum_fusion.1), channel_id=1, source_target_pairs={{0,16},{16,32},{32,48},{48,64},{64,80},{80,96},{96,112},{112,128},... | collective-permute-start | bytes 1572872 | tf_op jit(solution)/shard_map/ppermute | solution.py:22
  44.3 3.8 copy-start.7
  215.4 0.7 copy-start.10
  215.5 0.7 copy-start.11
  216.4 0.7 copy-start.2
  216.5 0.8 copy-start.6
  217.9 10.1 collective-permute-start.2
  220.1 7.9 collective-permute-start.3
  222.4 6.5 collective-permute-start.4
  228.0 22.5 %copy-start.3 = (bf16[128,1024]{1,0:T(8,128)(2,1)S(1)}, bf16[128,1024]{1,0:T(8,128)(2,1)}, u32[]{:S(2)}) copy-start(bf16[128,1024]{1,0:T(8,128)(2,1)} %copy-done.2) | copy-start | bytes 786436
Sparse Core Ops, SparseCore 0:
  12.7 67.5 all-gather.5
  83.6 59.9 all-gather.7
  257.5 763.0 all-gather.9
